TPU v7x, 32 devices: a whole 2x2x4 slice. The times are simulated.
32 devices in a mesh: section: 4 (over x, core), tp: 8 (over z, y).
Axes of the slice: x: 2, y: 2, z: 4, core: 2. Of those that a mesh axis runs over, the one named last changes fastest.
Arguments:
- gate_codes: bfloat16 [4, 96, 1280], P('section', None, 'tp'), may hold values from -128 to 127, as said below
- gate_exponents: int32 [4, 96, 40], P('section', None, 'tp'), may hold values from -8 to -6
- up_codes: bfloat16 [4, 96, 1280], P('section', None, 'tp'), may hold values from -128 to 127, as said below
- up_exponents: int32 [4, 96, 40], P('section', None, 'tp'), may hold values from -8 to -6
- down_codes: bfloat16 [4, 1280, 4096], P('section', 'tp'), may hold values from -128 to 127, as said below
- down_exponents: int32 [4, 40, 4096], P('section', 'tp'), may hold values from -14 to -12
- grad_held: bfloat16 [4, 96, 4096], P('section', 'tp'), may hold values from -6 to 6
Outputs:
- down_grad: bfloat16 [4, 1280, 4096], P('section', 'tp')
- gate_grad: bfloat16 [4, 96, 1280], P('section', None, 'tp')
- up_grad: bfloat16 [4, 96, 1280], P('section', None, 'tp')
Inputs may be any that keep to these rules, and one draw needn't show every extreme that they name: `gate_codes`: every entry is a whole number, independent of the others. `up_codes`: every entry is a whole number, independent of the others. `down_codes`: every entry is a whole number, independent of the others.
All inputs are finite; a program needn't handle non-finite values.
Results may differ from a plain program's by a relative error of at most 0.005.
Values may be sent and summed in bfloat16 or wider, within the bound.
No kernel may reach another device: no remote copies, remote signals or barrier semaphores. Data moves between devices by JAX's collectives and lax.ppermute only.
A program may use at most 64 MiB of HBM per device.

v0:
```python
import jax
import jax.numpy as jnp
from jax import lax
from jax.sharding import PartitionSpec as P


def shifted(shard, axis, by):
    count = lax.axis_size(axis)
    return lax.ppermute(shard, axis, [(i, (i + by) % count) for i in range(count)])


def dequantize(codes, exponents, target_axis):
    scales = jnp.exp2(jnp.repeat(exponents, 32, axis=target_axis).astype(jnp.float32))
    return (codes.astype(jnp.float32) * scales).astype(jnp.bfloat16)


def full_products(hidden, every_row, weight_rows):
    weight_sum = lax.dot_general(
        hidden, every_row, (((0,), (0,)), ((), ())), preferred_element_type=jnp.float32
    )
    hidden_slope = lax.dot_general(
        every_row, weight_rows, (((1,), (1,)), ((), ())), preferred_element_type=jnp.float32
    )
    return (weight_sum, hidden_slope)


def body(gate_codes, gate_exponents, up_codes, up_exponents, down_codes, down_exponents, grad_held):
    gate_value = dequantize(gate_codes[0], gate_exponents[0], 1)
    up_value = dequantize(up_codes[0], up_exponents[0], 1)
    weight_rows = dequantize(down_codes[0], down_exponents[0], 0)
    gate_wide = gate_value.astype(jnp.float32)
    up_wide = up_value.astype(jnp.float32)
    sigmoid_gate = jax.nn.sigmoid(gate_wide)
    silu_gate = gate_wide * sigmoid_gate
    hidden = (silu_gate * up_wide).astype(jnp.bfloat16)
    incoming_rows = grad_held[0]
    received = shifted(incoming_rows, "section", -1)
    every_row = lax.all_gather(received, "tp", axis=0, tiled=True)
    weight_sum, hidden_slope = full_products(hidden, every_row, weight_rows)
    gate_grad = (
        hidden_slope * up_wide * sigmoid_gate * (1.0 + gate_wide * (1.0 - sigmoid_gate))
    ).astype(jnp.bfloat16)
    up_grad = (hidden_slope * silu_gate).astype(jnp.bfloat16)
    return (weight_sum.astype(jnp.bfloat16)[None], gate_grad[None], up_grad[None])


def solution(mesh):
    placed = (
        P("section", None, "tp"),
        P("section", None, "tp"),
        P("section", None, "tp"),
        P("section", None, "tp"),
        P("section", "tp", None),
        P("section", "tp", None),
        P("section", "tp", None),
    )
    return jax.shard_map(
        body,
        mesh=mesh,
        in_specs=placed,
        out_specs=(P("section", "tp", None), P("section", None, "tp"), P("section", None, "tp")),
        check_vma=False,
    )
```

profile of v0, /device:TPU:0, one launch (start us, length us, event | category | flops | bytes accessed | tf_op | source)
XLA Modules:
  0.0 44.1 jit_solution(8253934703472863750)
XLA Ops:
  0.6 2.4 %collective-permute-start = (bf16[12,4096]{1,0:T(8,128)(2,1)}, bf16[12,4096]{1,0:T(8,128)(2,1)S(1)}, u32[]{:S(2)}, u32[]{:S(2)}) collective-permute-start(bf16[12,4096]{1,0:T(8,128)(2,1)} %bitcast.45), channel_id=1, source_target_pairs={{0,24},{8,0},{16,8},{24,16},{1,25},{9,1},{17,9},{25,17},{2,26},{10... | collective-permute-start | bytes 294920 | tf_op jit(solution)/shard_map/ppermute | solution.py:9
  3.1 0.7 %multiply_exponential_fusion.2 = f32[1,96,5]{1,0,2:T(1,128)S(1)} fusion(s32[1,96,5]{1,0,2:T(1,128)} %param.8), kind=kLoop, calls=%fused_computation.30 | loop fusion | flops 960 | bytes 3840 | tf_op jit(solution)/shard_map/exp2 | solution.py:13
  3.8 1.0 %multiply_exponential_fusion = f32[1,5,4096]{2,0,1:T(1,128)S(1)} fusion(s32[1,5,4096]{2,0,1:T(1,128)} %param.12), kind=kLoop, calls=%fused_computation.24 | loop fusion | flops 40960 | bytes 163840 | tf_op jit(solution)/shard_map/exp2 | solution.py:13
  4.8 0.7 %multiply_exponential_fusion.1 = f32[1,96,5]{1,0,2:T(1,128)S(1)} fusion(s32[1,96,5]{1,0,2:T(1,128)} %param.10), kind=kLoop, calls=%fused_computation.29 | loop fusion | flops 960 | bytes 3840 | tf_op jit(solution)/shard_map/exp2 | solution.py:13
  5.5 0.1 copy.16
  5.5 1.6 %fusion.1 = bf16[160,4096]{1,0:T(8,128)(2,1)S(1)} fusion(bf16[1,160,4096]{2,1,0:T(8,128)(2,1)} %param.11, f32[5,4096]{1,0:T(8,128)S(1)} %bitcast.41), kind=kLoop, calls=%fused_computation.3 | loop fusion | flops 1966080 | bytes 2703360 | tf_op jit(solution)/shard_map/convert_element_type | solution.py:14
  7.1 0.0 collective-permute-done
  7.1 33.1 %all-gather = bf16[8,12,4096]{2,1,0:T(8,128)(2,1)S(1)} all-gather(bf16[1,12,4096]{2,1,0:T(8,128)(2,1)S(1)} %bitcast.42), channel_id=1, replica_groups=mesh['section'=4,'tp'=8] {'tp'}, dimensions={0}, use_global_device_ids=true | all-gather | bytes 884736 | tf_op jit(solution)/shard_map/all_gather | solution.py:38
  40.3 0.2 reshape.43
  40.5 0.0 copy-start
  40.5 0.0 copy-start.1
  40.5 0.5 %convolution_bitcast_fusion = f32[96,160]{0,1:T(8,128)S(1)} fusion(bf16[160,4096]{1,0:T(8,128)(2,1)S(1)} %fusion.1, bf16[96,4096]{1,0:T(8,128)(2,1)S(1)} %reshape.43), kind=kOutput, calls=%fused_computation.4 | convolution fusion | flops 125829120 | bytes 2158592 | tf_op jit(solution)/shard_map/dot_general | solution.py:21
  41.0 0.3 copy-done
  41.2 0.7 %fusion.12 = (bf16[1,96,160]{1,2,0:T(8,128)(2,1)}, bf16[96,160]{0,1:T(8,128)(2,1)S(1)}) fusion(f32[96,160]{0,1:T(8,128)S(1)} %convolution_bitcast_fusion, f32[96,5]{0,1:T(8,128)S(1)} %bitcast.44, bf16[1,96,160]{1,2,0:T(8,128)(2,1)S(1)} %copy-done), kind=kLoop, calls=%fused_computation.25 | loop fusion | flops 153600 | bytes 155520 | tf_op jit(solution)/shard_map/broadcast_in_dim | solution.py:44
  41.9 0.0 copy-done.1
  41.9 0.7 %fusion.14 = (bf16[1,96,160]{1,2,0:T(8,128)(2,1)}, bf16[96,160]{0,1:T(8,128)(2,1)S(1)}) fusion(bf16[96,160]{0,1:T(8,128)(2,1)S(1)} %get-tuple-element.4, f32[96,160]{0,1:T(8,128)S(1)} %convolution_bitcast_fusion, f32[96,5]{0,1:T(8,128)S(1)} %bitcast.43, bf16[1,96,160]{1,2,0:T(8,128)(2,1)S(1)} %copy-done.1), kind=kLoop, calls=%fused_computation.26 | loop fusion | flops 230400 | bytes 186240 | tf_op jit(solution)/shard_map/broadcast_in_dim | solution.py:44
  42.6 1.6 %fusion = bf16[1,160,4096]{2,1,0:T(8,128)(2,1)} fusion(bf16[96,4096]{1,0:T(8,128)(2,1)S(1)} %reshape.43, bf16[96,160]{0,1:T(8,128)(2,1)S(1)} %get-tuple-element.6, bf16[96,160]{0,1:T(8,128)(2,1)S(1)} %get-tuple-element.4), kind=kOutput, calls=%fused_computation.1 | convolution fusion | flops 126607360 | bytes 2158592 | tf_op jit(solution)/shard_map/dot_general | solution.py:18
  (2 shorter events, 0.0 us)
Async XLA Ops:
  0.6 6.5 %collective-permute-start = (bf16[12,4096]{1,0:T(8,128)(2,1)}, bf16[12,4096]{1,0:T(8,128)(2,1)S(1)}, u32[]{:S(2)}, u32[]{:S(2)}) collective-permute-start(bf16[12,4096]{1,0:T(8,128)(2,1)} %bitcast.45), channel_id=1, source_target_pairs={{0,24},{8,0},{16,8},{24,16},{1,25},{9,1},{17,9},{25,17},{2,26},{10... | collective-permute-start | bytes 294920 | tf_op jit(solution)/shard_map/ppermute | solution.py:9
  40.5 0.8 %copy-start = (bf16[1,96,160]{1,2,0:T(8,128)(2,1)S(1)}, bf16[1,96,160]{1,2,0:T(8,128)(2,1)}, u32[]{:S(2)}) copy-start(bf16[1,96,160]{1,2,0:T(8,128)(2,1)} %param.7) | copy-start | bytes 92164
  40.5 1.4 %copy-start.1 = (bf16[1,96,160]{1,2,0:T(8,128)(2,1)S(1)}, bf16[1,96,160]{1,2,0:T(8,128)(2,1)}, u32[]{:S(2)}) copy-start(bf16[1,96,160]{1,2,0:T(8,128)(2,1)} %param.9) | copy-start | bytes 92164
where the time goes:
time: 44.4 us; the launch traced here: 44.1 us
  blocking collectives  33.1 us (75%)
  other arithmetic  5.3 us (12%)
  starting transfers between devices  2.43 us (5%)
  matrix products  2.04 us (5%)
  between operations  0.71 us (2%)
  local copies, waits for them, and re-layouts  0.5 us (1%)
    all_gather x1, blocking collectives, body(): every_row = lax.all_gather(received, 'tp', axis=0, tiled=True)  33.1 us
    ppermute x1, starting transfers between devices, shifted(): lax.ppermute(shard, axis, [(i, (i + by) % count) for i in range(count)])  2.43 us
    exp2 x3, other arithmetic, dequantize(): jnp.exp2(jnp.repeat(exponents, 32, axis=target_axis).astype(jnp.float32))  2.39 us
    convert_element_type x1, other arithmetic, dequantize(): return (codes.astype(jnp.float32) * scales).astype(jnp.bfloat16)  1.58 us
    dot_general x1, matrix products, full_products(): lax.dot_general(hidden, every_row, (((0,), (0,)), ((), ())), preferred_el...  1.55 us
  transfers between devices with their start and end apart: 1, of which 0 were waited for; matrix products, arithmetic and copies ran while one was open for 9% of the time, Pallas kernels for 0%

commit v1 on v0

v1 whole, which is shorter than its diff:
```python
import jax
import jax.numpy as jnp
from jax import lax
from jax.sharding import PartitionSpec as P

TILE = 16


def dequantize(codes, exponents, target_axis):
    per = codes.shape[target_axis] // exponents.shape[target_axis]
    scales = jnp.exp2(jnp.repeat(exponents, per, axis=target_axis).astype(jnp.float32))
    return (codes.astype(jnp.float32) * scales).astype(jnp.bfloat16)


def send(array, flip, hop):
    sections, count = lax.axis_size("section"), lax.axis_size("tp")
    if hop == 0:
        return lax.ppermute(array, "tp", [(t, t ^ flip) for t in range(count)])
    pairs = [
        (s * count + t, ((s - hop) % sections) * count + (t ^ flip))
        for s in range(sections)
        for t in range(count)
    ]
    return lax.ppermute(array, ("section", "tp"), pairs)


def packed(rows):
    count, width = rows.shape
    free = TILE - count
    keep = width * count // TILE
    parts = count // free
    tail = rows[:, keep:].reshape(parts, free, width - keep)
    low = tail.transpose(1, 0, 2).reshape(free, keep)
    return jnp.concatenate([rows[:, :keep], low], axis=0)


def unpacked(slots, count, width):
    free = TILE - count
    keep = width * count // TILE
    parts = count // free
    number = slots.shape[0]
    low = slots[:, count:, :].reshape(number, free, parts, width - keep)
    tail = low.transpose(0, 2, 1, 3).reshape(number, count, width - keep)
    return jnp.concatenate([slots[:, :count, :], tail], axis=2)


def gathered(rows):
    count, width = rows.shape
    n = lax.axis_size("tp")
    p = packed(rows)
    got = {}
    for flip in sorted([f for f in range(n) if f % 2 == 0 and f > 0], reverse=True):
        got[flip] = send(p, flip, 1)
    got[0] = send(p, 0, 1)
    got[1] = send(p, 1, 1)
    for flip in range(2, n, 2):
        got[flip + 1] = send(got[flip], 1, 0)
    return unpacked(jnp.stack([got[j] for j in range(n)]), count, width)


def body(gate_codes, gate_exponents, up_codes, up_exponents, down_codes, down_exponents, grad_held):
    n = lax.axis_size("tp")
    rows, width = grad_held.shape[1:]
    gate_value = dequantize(gate_codes[0], gate_exponents[0], 1)
    up_value = dequantize(up_codes[0], up_exponents[0], 1)
    weight_rows = dequantize(down_codes[0], down_exponents[0], 0)
    if n & (n - 1) == 0 and n <= TILE:
        order = jnp.bitwise_xor(lax.axis_index("tp"), jnp.arange(n))
        every_row = gathered(grad_held[0]).reshape(n * rows, width)
    else:
        order = jnp.arange(n)
        count = lax.axis_size("section")
        received = lax.ppermute(grad_held[0], "section", [(i, (i - 1) % count) for i in range(count)])
        every_row = lax.all_gather(received, "tp", axis=0, tiled=True)

    def reordered(array):
        return array.reshape(n, rows, -1)[order].reshape(array.shape)

    gate_wide = reordered(gate_value).astype(jnp.float32)
    up_wide = reordered(up_value).astype(jnp.float32)
    sigmoid_gate = jax.nn.sigmoid(gate_wide)
    silu_gate = gate_wide * sigmoid_gate
    hidden = (silu_gate * up_wide).astype(jnp.bfloat16)
    down_grad = lax.dot_general(
        hidden, every_row, (((0,), (0,)), ((), ())), preferred_element_type=jnp.float32
    )
    slope = lax.dot_general(
        every_row, weight_rows, (((1,), (1,)), ((), ())), preferred_element_type=jnp.float32
    )
    gate_grad = (slope * up_wide * sigmoid_gate * (1.0 + gate_wide * (1.0 - sigmoid_gate))).astype(jnp.bfloat16)
    up_grad = (slope * silu_gate).astype(jnp.bfloat16)
    return (down_grad.astype(jnp.bfloat16)[None], reordered(gate_grad)[None], reordered(up_grad)[None])


def solution(mesh):
    placed = (
        P("section", None, "tp"),
        P("section", None, "tp"),
        P("section", None, "tp"),
        P("section", None, "tp"),
        P("section", "tp", None),
        P("section", "tp", None),
        P("section", "tp", None),
    )
    return jax.shard_map(
        body,
        mesh=mesh,
        in_specs=placed,
        out_specs=(P("section", "tp", None), P("section", None, "tp"), P("section", None, "tp")),
        check_vma=False,
    )
```

time: 44.4 us -> 33.4 us (0.75)
  blocking collectives: 33.1 us -> 0 us
  local copies, waits for them, and re-layouts: 0.5 us -> 13.2 us
  starting transfers between devices: 2.43 us -> 11.3 us
  waiting for transfers between devices: 0.01 us -> 3.62 us
  other arithmetic: 5.3 us -> 1.81 us
    all_gather x1 -> x0, blocking collectives: 33.1 us -> none  [body(): every_row = lax.all_gather(received, 'tp', axis=0, tiled=True)]
    ppermute x1 -> x8, starting transfers between devices: 2.43 us -> 11.3 us  [the longest x5 8.62 us: send(): return lax.ppermute(array, ('section', 'tp'), pairs)]
    unnamed x8 -> x23, local copies, waits for them, and re-layouts: 0.5 us -> 6.32 us
    ppermute x1 -> x8, waiting for transfers between devices: 0.01 us -> 3.62 us  [the longest x3 3.61 us: send(): return lax.ppermute(array, 'tp', [(t, t ^ flip) for t in range(count)])]
    gather x0 -> x4, local copies, waits for them, and re-layouts: none -> 2.21 us  [reordered(): return array.reshape(n, rows, -1)[order].reshape(array.shape)]
    slice x0 -> x4, local copies, waits for them, and re-layouts: none -> 1.84 us  [the longest x1 0.92 us: packed(): return jnp.concatenate([rows[:, :keep], low], axis=0)]
    exp2 x3, other arithmetic: 2.39 us -> 0.82 us  [dequantize(): jnp.exp2(jnp.repeat(exponents, per, axis=target_axis).astype(jnp.float32))]
    broadcast_in_dim x2 -> x0, other arithmetic: 1.33 us -> none  [the longest x1 0.67 us: body(): gate_grad[None]]
  transfers between devices with their start and end apart: 1 -> 8, of which waited for: 0 -> 3; matrix products, arithmetic and copies ran while one was open for 9% -> 26% of each run, Pallas kernels for 0% -> 0%
where the time goes in v1:
time: 33.4 us; the launch traced here: 33 us
  local copies, waits for them, and re-layouts  13.2 us (40%)
  starting transfers between devices  11.3 us (34%)
  waiting for transfers between devices  3.62 us (11%)
  matrix products  2.04 us (6%)
  other arithmetic  1.81 us (5%)
  between operations  1 us (3%)
    ppermute x5, starting transfers between devices, send(): return lax.ppermute(array, ('section', 'tp'), pairs)  8.62 us
    unnamed x23, local copies, waits for them, and re-layouts  6.32 us
    ppermute x3, waiting for transfers between devices, send(): return lax.ppermute(array, 'tp', [(t, t ^ flip) for t in range(count)])  3.61 us
    ppermute x3, starting transfers between devices, send(): return lax.ppermute(array, 'tp', [(t, t ^ flip) for t in range(count)])  2.66 us
    gather x4, local copies, waits for them, and re-layouts, reordered(): return array.reshape(n, rows, -1)[order].reshape(array.shape)  2.21 us
    dot_general x1, matrix products, body(): lax.dot_general(hidden, every_row, (((0,), (0,)), ((), ())), preferred_el...  1.55 us
    slice x1, local copies, waits for them, and re-layouts, packed(): return jnp.concatenate([rows[:, :keep], low], axis=0)  0.92 us
    exp2 x3, other arithmetic, dequantize(): jnp.exp2(jnp.repeat(exponents, per, axis=target_axis).astype(jnp.float32))  0.82 us
  transfers between devices with their start and end apart: 8, of which 3 were waited for; matrix products, arithmetic and copies ran while one was open for 26% of the time, Pallas kernels for 0%

profile of v1, /device:TPU:0, one launch (start us, length us, event | category | flops | bytes accessed | tf_op | source)
XLA Modules:
  0.0 33.0 jit_solution(1799388048765737813)
XLA Ops:
  0.6 0.0 copy-start.3
  0.6 0.0 copy-start.5
  0.6 0.9 %slice.24 = bf16[12,3072]{1,0:T(8,128)(2,1)S(1)} slice(bf16[12,4096]{1,0:T(8,128)(2,1)} %bitcast.46), slice={[0:12], [0:3072]} | slice | bytes 147456 | tf_op jit(solution)/shard_map/slice | solution.py:34
  1.6 0.8 %slice.25 = bf16[12,1024]{1,0:T(8,128)(2,1)S(1)} slice(bf16[12,4096]{1,0:T(8,128)(2,1)} %bitcast.47), slice={[0:12], [3072:4096]} | slice | bytes 49152 | tf_op jit(solution)/shard_map/slice | solution.py:32
  2.3 0.0 copy-start.4
  2.4 0.7 %pad_maximum_fusion = bf16[16,3072]{1,0:T(8,128)(2,1)} fusion(bf16[4,3072]{1,0:T(4,128)(2,1)S(1)} %bitcast.48, bf16[12,3072]{1,0:T(8,128)(2,1)S(1)} %slice.24), kind=kLoop, calls=%fused_computation.11 | loop fusion | flops 196608 | bytes 196608 | tf_op jit(solution)/shard_map/concatenate | solution.py:34
  3.0 2.4 %collective-permute-start = (bf16[16,3072]{1,0:T(8,128)(2,1)}, bf16[16,3072]{1,0:T(8,128)(2,1)}, u32[]{:S(2)}, u32[]{:S(2)}) collective-permute-start(bf16[16,3072]{1,0:T(8,128)(2,1)} %pad_maximum_fusion), channel_id=1, source_target_pairs={{0,24},{1,25},{2,26},{3,27},{4,28},{5,29},{6,30},{7,31},{8,0},{9,1... | collective-permute-start | bytes 294920 | tf_op jit(solution)/shard_map/ppermute | solution.py:24
  5.4 1.6 %collective-permute-start.1 = (bf16[16,3072]{1,0:T(8,128)(2,1)}, bf16[16,3072]{1,0:T(8,128)(2,1)}, u32[]{:S(2)}, u32[]{:S(2)}) collective-permute-start(bf16[16,3072]{1,0:T(8,128)(2,1)} %pad_maximum_fusion), channel_id=1, source_target_pairs={{0,25},{1,24},{2,27},{3,26},{4,29},{5,28},{6,31},{7,30},{8,1},{9,0... | collective-permute-start | bytes 294920 | tf_op jit(solution)/shard_map/ppermute | solution.py:24
  7.0 1.2 %collective-permute-start.2 = (bf16[16,3072]{1,0:T(8,128)(2,1)}, bf16[16,3072]{1,0:T(8,128)(2,1)}, u32[]{:S(2)}, u32[]{:S(2)}) collective-permute-start(bf16[16,3072]{1,0:T(8,128)(2,1)} %pad_maximum_fusion), channel_id=1, source_target_pairs={{0,26},{1,27},{2,24},{3,25},{4,30},{5,31},{6,28},{7,29},{8,2},{9,3... | collective-permute-start | bytes 294920 | tf_op jit(solution)/shard_map/ppermute | solution.py:24
  8.2 2.7 %collective-permute-start.4 = (bf16[16,3072]{1,0:T(8,128)(2,1)}, bf16[16,3072]{1,0:T(8,128)(2,1)}, u32[]{:S(2)}, u32[]{:S(2)}) collective-permute-start(bf16[16,3072]{1,0:T(8,128)(2,1)} %pad_maximum_fusion), channel_id=1, source_target_pairs={{0,28},{1,29},{2,30},{3,31},{4,24},{5,25},{6,26},{7,27},{8,4},{9,5... | collective-permute-start | bytes 294920 | tf_op jit(solution)/shard_map/ppermute | solution.py:24
  10.9 0.8 %collective-permute-start.6 = (bf16[16,3072]{1,0:T(8,128)(2,1)}, bf16[16,3072]{1,0:T(8,128)(2,1)}, u32[]{:S(2)}, u32[]{:S(2)}) collective-permute-start(bf16[16,3072]{1,0:T(8,128)(2,1)} %pad_maximum_fusion), channel_id=1, source_target_pairs={{0,30},{1,31},{2,28},{3,29},{4,26},{5,27},{6,24},{7,25},{8,6},{9,7... | collective-permute-start | bytes 294920 | tf_op jit(solution)/shard_map/ppermute | solution.py:24
  11.7 0.7 %multiply_exponential_fusion.2 = f32[1,96,5]{1,0,2:T(1,128)S(1)} fusion(s32[1,96,5]{1,0,2:T(1,128)} %param.8), kind=kLoop, calls=%fused_computation.31 | loop fusion | flops 960 | bytes 3840 | tf_op jit(solution)/shard_map/exp2 | solution.py:11
  12.4 0.1 copy.25
  12.5 0.2 broadcast_in_dim.16
  12.6 0.1 exp2.58
  12.8 0.0 copy-done.3
  12.8 0.1 copy.10
  12.9 0.0 copy-done.5
  12.9 0.1 copy.26
  13.0 0.2 broadcast_in_dim.17
  13.2 0.0 copy-start
  13.2 0.1 exp2.62
  13.4 0.1 copy.14
  13.5 0.0 copy-done.2
  13.5 0.1 multiply_exponential_fusion
  13.7 0.6 %gather_fusion = bf16[8,12,160]{2,1,0:T(8,128)(2,1)S(1)} fusion(bf16[8,12,160]{2,1,0:T(8,128)(2,1)S(1)} %multiply_convert_fusion.1, s32[1024]{0:T(1024)S(1)} %pad_clamp_fusion), kind=kCustom, calls=%fused_computation | custom fusion | bytes 61472 | tf_op jit(solution)/shard_map/gather | solution.py:77
  14.3 0.1 copy.13
  14.4 0.6 %gather_fusion.1 = bf16[8,12,160]{2,1,0:T(8,128)(2,1)S(1)} fusion(bf16[8,12,160]{2,1,0:T(8,128)(2,1)S(1)} %multiply_convert_fusion, s32[1024]{0:T(1024)S(1)} %pad_clamp_fusion), kind=kCustom, calls=%fused_computation.1 | custom fusion | bytes 61472 | tf_op jit(solution)/shard_map/gather | solution.py:77
  15.0 0.7 %copy.16 = f32[96,160]{0,1:T(8,128)} copy(f32[96,160]{1,0:T(8,128)S(1)} %reshape.95) | data formatting | bytes 122880 | tf_op jit(solution)/shard_map/convert_element_type | solution.py:80
  15.7 0.1 copy.29
  15.7 0.0 copy-done
  15.7 0.3 fusion.1
  16.0 0.0 collective-permute-done
  16.0 0.9 %bitcast_dynamic-update-slice_fusion.7 = bf16[8,16,3072]{2,1,0:T(8,128)(2,1)S(1)} fusion(bf16[16,3072]{1,0:T(8,128)(2,1)} %collective-permute-done), kind=kLoop, calls=%fused_computation.19 | loop fusion | bytes 196608
  16.9 0.0 collective-permute-done.2
  16.9 0.6 %collective-permute-start.3 = (bf16[16,3072]{1,0:T(8,128)(2,1)}, bf16[16,3072]{1,0:T(8,128)(2,1)S(1)}, u32[]{:S(2)}, u32[]{:S(2)}) collective-permute-start(bf16[16,3072]{1,0:T(8,128)(2,1)} %collective-permute-done.2), channel_id=1, source_target_pairs={{0,1},{1,0},{2,3},{3,2},{4,5},{5,4},{6,7},{7,6},{8,9},{9,8},{10,11... | collective-permute-start | bytes 294920 | tf_op jit(solution)/shard_map/ppermute | solution.py:18
  17.5 0.0 collective-permute-done.1
  17.5 0.9 %bitcast_dynamic-update-slice_fusion.6 = bf16[8,16,3072]{2,1,0:T(8,128)(2,1)S(1)} fusion(bf16[8,16,3072]{2,1,0:T(8,128)(2,1)S(1)} %bitcast_dynamic-update-slice_fusion.7, bf16[16,3072]{1,0:T(8,128)(2,1)} %collective-permute-done.1), kind=kLoop, calls=%fused_computation.18 | loop fusion | bytes 196608
  18.4 0.9 %bitcast_dynamic-update-slice_fusion.5 = bf16[8,16,3072]{2,1,0:T(8,128)(2,1)S(1)} fusion(bf16[8,16,3072]{2,1,0:T(8,128)(2,1)S(1)} %bitcast_dynamic-update-slice_fusion.6, bf16[16,3072]{1,0:T(8,128)(2,1)} %collective-permute-done.2), kind=kLoop, calls=%fused_computation.17 | loop fusion | bytes 196608
  19.3 0.0 collective-permute-done.4
  19.3 1.6 %collective-permute-start.5 = (bf16[16,3072]{1,0:T(8,128)(2,1)}, bf16[16,3072]{1,0:T(8,128)(2,1)S(1)}, u32[]{:S(2)}, u32[]{:S(2)}) collective-permute-start(bf16[16,3072]{1,0:T(8,128)(2,1)} %collective-permute-done.4), channel_id=1, source_target_pairs={{0,1},{1,0},{2,3},{3,2},{4,5},{5,4},{6,7},{7,6},{8,9},{9,8},{10,11... | collective-permute-start | bytes 294920 | tf_op jit(solution)/shard_map/ppermute | solution.py:18
  20.9 0.0 collective-permute-done.6
  20.9 0.5 %collective-permute-start.7 = (bf16[16,3072]{1,0:T(8,128)(2,1)}, bf16[16,3072]{1,0:T(8,128)(2,1)S(1)}, u32[]{:S(2)}, u32[]{:S(2)}) collective-permute-start(bf16[16,3072]{1,0:T(8,128)(2,1)} %collective-permute-done.6), channel_id=1, source_target_pairs={{0,1},{1,0},{2,3},{3,2},{4,5},{5,4},{6,7},{7,6},{8,9},{9,8},{10,11... | collective-permute-start | bytes 294920 | tf_op jit(solution)/shard_map/ppermute | solution.py:18
  21.4 0.4 %collective-permute-done.3 = bf16[16,3072]{1,0:T(8,128)(2,1)S(1)} collective-permute-done((bf16[16,3072]{1,0:T(8,128)(2,1)}, bf16[16,3072]{1,0:T(8,128)(2,1)S(1)}, u32[]{:S(2)}, u32[]{:S(2)}) %collective-permute-start.3) | collective-permute-done | bytes 98336 | tf_op jit(solution)/shard_map/ppermute | solution.py:18
  21.8 0.9 %bitcast_dynamic-update-slice_fusion.3 = bf16[8,16,3072]{2,1,0:T(8,128)(2,1)S(1)} fusion(bf16[8,16,3072]{2,1,0:T(8,128)(2,1)S(1)} %bitcast_dynamic-update-slice_fusion.4, bf16[16,3072]{1,0:T(8,128)(2,1)} %collective-permute-done.4), kind=kLoop, calls=%fused_computation.15 | loop fusion | bytes 196608
  22.7 2.5 %collective-permute-done.5 = bf16[16,3072]{1,0:T(8,128)(2,1)S(1)} collective-permute-done((bf16[16,3072]{1,0:T(8,128)(2,1)}, bf16[16,3072]{1,0:T(8,128)(2,1)S(1)}, u32[]{:S(2)}, u32[]{:S(2)}) %collective-permute-start.5) | collective-permute-done | bytes 98336 | tf_op jit(solution)/shard_map/ppermute | solution.py:18
  25.2 0.9 %bitcast_dynamic-update-slice_fusion.1 = bf16[8,16,3072]{2,1,0:T(8,128)(2,1)S(1)} fusion(bf16[8,16,3072]{2,1,0:T(8,128)(2,1)S(1)} %bitcast_dynamic-update-slice_fusion.2, bf16[16,3072]{1,0:T(8,128)(2,1)} %collective-permute-done.6), kind=kLoop, calls=%fused_computation.13 | loop fusion | bytes 196608
  26.1 0.7 %collective-permute-done.7 = bf16[16,3072]{1,0:T(8,128)(2,1)S(1)} collective-permute-done((bf16[16,3072]{1,0:T(8,128)(2,1)}, bf16[16,3072]{1,0:T(8,128)(2,1)S(1)}, u32[]{:S(2)}, u32[]{:S(2)}) %collective-permute-start.7) | collective-permute-done | bytes 98336 | tf_op jit(solution)/shard_map/ppermute | solution.py:18
  26.9 0.1 slice.27
  27.0 0.1 concatenate.12
  27.2 0.0 copy-start.1
  27.2 0.1 copy.17
  27.2 0.3 reshape.89
  27.5 0.2 copy.18
  27.7 0.1 concatenate.13
  27.8 0.2 copy-done.1
  28.0 1.5 %fusion = bf16[1,160,4096]{2,1,0:T(8,128)(2,1)} fusion(bf16[96,4096]{1,0:T(8,128)(2,1)S(1)} %constant_dynamic-update-slice_fusion, f32[96,160]{0,1:T(8,128)S(1)} %copy-done.1, f32[96,160]{0,1:T(8,128)S(1)} %copy.13), kind=kOutput, calls=%fused_computation.5 | convolution fusion | flops 126576640 | bytes 2220032 | tf_op jit(solution)/shard_map/dot_general | solution.py:84
  29.6 0.5 %multiply_convert_fusion.2 = (bf16[96,160]{0,1:T(8,128)(2,1)S(1)}, bf16[96,160]{0,1:T(8,128)(2,1)S(1)}) fusion(f32[96,160]{0,1:T(8,128)S(1)} %copy.13, f32[96,160]{0,1:T(8,128)S(1)} %copy-done.1, bf16[96,4096]{1,0:T(8,128)(2,1)S(1)} %constant_dynamic-update-slice_fusion, bf16[160,4096]{1,0:T(8,128)(2,1)S(1)} %fusion.1), kind=kOutput, calls=%fused_computation.20 | convolution fusion | flops 126028800 | bytes 2281472 | tf_op jit(solution)/shard_map/dot_general | solution.py:87
  30.1 0.1 copy.21
  30.2 0.6 %gather_fusion.2 = bf16[8,12,160]{2,1,0:T(8,128)(2,1)S(1)} fusion(bf16[8,12,160]{2,1,0:T(8,128)(2,1)S(1)} %reshape.90, s32[1024]{0:T(1024)S(1)} %pad_clamp_fusion), kind=kCustom, calls=%fused_computation.2 | custom fusion | bytes 61472 | tf_op jit(solution)/shard_map/gather | solution.py:77
  30.8 0.7 %copy.23 = bf16[1,96,160]{1,2,0:T(8,128)(2,1)} copy(bf16[1,96,160]{2,1,0:T(8,128)(2,1)S(1)} %broadcast_in_dim_reshape.6) | data formatting | bytes 61440
  31.5 0.1 copy.22
  31.7 0.6 %gather_fusion.3 = bf16[8,12,160]{2,1,0:T(8,128)(2,1)S(1)} fusion(bf16[8,12,160]{2,1,0:T(8,128)(2,1)S(1)} %reshape.91, s32[1024]{0:T(1024)S(1)} %pad_clamp_fusion), kind=kCustom, calls=%fused_computation.3 | custom fusion | bytes 61472 | tf_op jit(solution)/shard_map/gather | solution.py:77
  32.2 0.7 %copy.24 = bf16[1,96,160]{1,2,0:T(8,128)(2,1)} copy(bf16[1,96,160]{2,1,0:T(8,128)(2,1)S(1)} %broadcast_in_dim_reshape.7) | data formatting | bytes 61440
  (21 shorter events, 0.3 us)
Async XLA Ops:
  0.6 12.1 %copy-start.3 = (bf16[1,96,160]{1,2,0:T(8,128)(2,1)S(1)}, bf16[1,96,160]{1,2,0:T(8,128)(2,1)}, u32[]{:S(2)}) copy-start(bf16[1,96,160]{1,2,0:T(8,128)(2,1)} %param.7) | copy-start | bytes 92164
  0.6 12.3 %copy-start.5 = (s32[1,96,5]{1,0,2:T(1,128)S(1)}, s32[1,96,5]{1,0,2:T(1,128)}, u32[]{:S(2)}) copy-start(s32[1,96,5]{1,0,2:T(1,128)} %param.10) | copy-start | bytes 5764
  2.3 11.0 %copy-start.4 = (bf16[1,96,160]{1,2,0:T(8,128)(2,1)S(1)}, bf16[1,96,160]{1,2,0:T(8,128)(2,1)}, u32[]{:S(2)}) copy-start(bf16[1,96,160]{1,2,0:T(8,128)(2,1)} %param.9) | copy-start | bytes 92164
  3.0 13.0 %collective-permute-start = (bf16[16,3072]{1,0:T(8,128)(2,1)}, bf16[16,3072]{1,0:T(8,128)(2,1)}, u32[]{:S(2)}, u32[]{:S(2)}) collective-permute-start(bf16[16,3072]{1,0:T(8,128)(2,1)} %pad_maximum_fusion), channel_id=1, source_target_pairs={{0,24},{1,25},{2,26},{3,27},{4,28},{5,29},{6,30},{7,31},{8,0},{9,1... | collective-permute-start | bytes 294920 | tf_op jit(solution)/shard_map/ppermute | solution.py:24
  5.4 12.1 %collective-permute-start.1 = (bf16[16,3072]{1,0:T(8,128)(2,1)}, bf16[16,3072]{1,0:T(8,128)(2,1)}, u32[]{:S(2)}, u32[]{:S(2)}) collective-permute-start(bf16[16,3072]{1,0:T(8,128)(2,1)} %pad_maximum_fusion), channel_id=1, source_target_pairs={{0,25},{1,24},{2,27},{3,26},{4,29},{5,28},{6,31},{7,30},{8,1},{9,0... | collective-permute-start | bytes 294920 | tf_op jit(solution)/shard_map/ppermute | solution.py:24
  7.0 9.9 %collective-permute-start.2 = (bf16[16,3072]{1,0:T(8,128)(2,1)}, bf16[16,3072]{1,0:T(8,128)(2,1)}, u32[]{:S(2)}, u32[]{:S(2)}) collective-permute-start(bf16[16,3072]{1,0:T(8,128)(2,1)} %pad_maximum_fusion), channel_id=1, source_target_pairs={{0,26},{1,27},{2,24},{3,25},{4,30},{5,31},{6,28},{7,29},{8,2},{9,3... | collective-permute-start | bytes 294920 | tf_op jit(solution)/shard_map/ppermute | solution.py:24
  8.2 11.1 %collective-permute-start.4 = (bf16[16,3072]{1,0:T(8,128)(2,1)}, bf16[16,3072]{1,0:T(8,128)(2,1)}, u32[]{:S(2)}, u32[]{:S(2)}) collective-permute-start(bf16[16,3072]{1,0:T(8,128)(2,1)} %pad_maximum_fusion), channel_id=1, source_target_pairs={{0,28},{1,29},{2,30},{3,31},{4,24},{5,25},{6,26},{7,27},{8,4},{9,5... | collective-permute-start | bytes 294920 | tf_op jit(solution)/shard_map/ppermute | solution.py:24
  10.9 10.0 %collective-permute-start.6 = (bf16[16,3072]{1,0:T(8,128)(2,1)}, bf16[16,3072]{1,0:T(8,128)(2,1)}, u32[]{:S(2)}, u32[]{:S(2)}) collective-permute-start(bf16[16,3072]{1,0:T(8,128)(2,1)} %pad_maximum_fusion), channel_id=1, source_target_pairs={{0,30},{1,31},{2,28},{3,29},{4,26},{5,27},{6,24},{7,25},{8,6},{9,7... | collective-permute-start | bytes 294920 | tf_op jit(solution)/shard_map/ppermute | solution.py:24
  12.5 1.0 %copy-start.2 = (s32[1,5,4096]{2,0,1:T(1,128)S(1)}, s32[1,5,4096]{2,0,1:T(1,128)}, u32[]{:S(2)}) copy-start(s32[1,5,4096]{2,0,1:T(1,128)} %param.12) | copy-start | bytes 245764
  13.2 2.5 %copy-start = (bf16[1,160,4096]{2,1,0:T(8,128)(2,1)S(1)}, bf16[1,160,4096]{2,1,0:T(8,128)(2,1)}, u32[]{:S(2)}) copy-start(bf16[1,160,4096]{2,1,0:T(8,128)(2,1)} %param.11) | copy-start | bytes 3932164
  16.9 4.9 %collective-permute-start.3 = (bf16[16,3072]{1,0:T(8,128)(2,1)}, bf16[16,3072]{1,0:T(8,128)(2,1)S(1)}, u32[]{:S(2)}, u32[]{:S(2)}) collective-permute-start(bf16[16,3072]{1,0:T(8,128)(2,1)} %collective-permute-done.2), channel_id=1, source_target_pairs={{0,1},{1,0},{2,3},{3,2},{4,5},{5,4},{6,7},{7,6},{8,9},{9,8},{10,11... | collective-permute-start | bytes 294920 | tf_op jit(solution)/shard_map/ppermute | solution.py:18
  19.3 5.9 %collective-permute-start.5 = (bf16[16,3072]{1,0:T(8,128)(2,1)}, bf16[16,3072]{1,0:T(8,128)(2,1)S(1)}, u32[]{:S(2)}, u32[]{:S(2)}) collective-permute-start(bf16[16,3072]{1,0:T(8,128)(2,1)} %collective-permute-done.4), channel_id=1, source_target_pairs={{0,1},{1,0},{2,3},{3,2},{4,5},{5,4},{6,7},{7,6},{8,9},{9,8},{10,11... | collective-permute-start | bytes 294920 | tf_op jit(solution)/shard_map/ppermute | solution.py:18
  20.9 5.9 %collective-permute-start.7 = (bf16[16,3072]{1,0:T(8,128)(2,1)}, bf16[16,3072]{1,0:T(8,128)(2,1)S(1)}, u32[]{:S(2)}, u32[]{:S(2)}) collective-permute-start(bf16[16,3072]{1,0:T(8,128)(2,1)} %collective-permute-done.6), channel_id=1, source_target_pairs={{0,1},{1,0},{2,3},{3,2},{4,5},{5,4},{6,7},{7,6},{8,9},{9,8},{10,11... | collective-permute-start | bytes 294920 | tf_op jit(solution)/shard_map/ppermute | solution.py:18
  27.2 0.9 %copy-start.1 = (f32[96,160]{0,1:T(8,128)S(1)}, f32[96,160]{0,1:T(8,128)}, u32[]{:S(2)}) copy-start(f32[96,160]{0,1:T(8,128)} %copy.16) | copy-start | bytes 184324

commit v2 on v0

v2 whole, which is shorter than its diff:
```python
import functools

import jax
import jax.numpy as jnp
from jax import lax
from jax.experimental import pallas as pl
from jax.experimental.pallas import tpu as pltpu
from jax.sharding import PartitionSpec as P

TILE = 16
WHOLE = pl.BlockSpec(memory_space=pltpu.VMEM)
LEFT = pl.BlockSpec(memory_space=pltpu.HBM)
PARAMS = pltpu.CompilerParams(vmem_limit_bytes=24 * 1024 * 1024)


def send(array, flip, hop):
    sections, count = lax.axis_size("section"), lax.axis_size("tp")
    if hop == 0:
        return lax.ppermute(array, "tp", [(t, t ^ flip) for t in range(count)])
    pairs = [
        (s * count + t, ((s - hop) % sections) * count + (t ^ flip))
        for s in range(sections)
        for t in range(count)
    ]
    return lax.ppermute(array, ("section", "tp"), pairs)


def fetched(refs, held_refs, sems):
    copies = [pltpu.make_async_copy(ref, held, sems.at[i]) for i, (ref, held) in enumerate(zip(refs, held_refs))]
    for copy in copies:
        copy.start()
    return copies


def pack_kernel(held_ref, packed_ref, rows_ref, sems):
    for copy in fetched([held_ref], [rows_ref], sems):
        copy.wait()
    count, width = rows_ref.shape
    free = TILE - count
    keep = width * count // TILE
    rows = rows_ref[...]
    parts = [rows[at : at + free, keep:] for at in range(0, count, free)]
    packed_ref[...] = jnp.concatenate([rows[:, :keep], jnp.concatenate(parts, axis=1)], axis=0)


def pack(rows):
    count, width = rows.shape
    return pl.pallas_call(
        pack_kernel,
        out_shape=pltpu.VMEM((TILE, width * count // TILE), jnp.bfloat16),
        in_specs=[LEFT],
        out_specs=WHOLE,
        scratch_shapes=[pltpu.VMEM(rows.shape, rows.dtype), pltpu.SemaphoreType.DMA((1,))],
        compiler_params=PARAMS,
    )(pltpu.with_memory_space_constraint(rows, pltpu.HBM))


def spread(tokens, slots, count, position):
    shape = (tokens, slots * TILE)
    lane = lax.broadcasted_iota(jnp.int32, shape, 1)
    row = lane & (TILE - 1)
    token = ((lane >> (TILE.bit_length() - 1)) ^ position) * count + row
    hit = (lax.broadcasted_iota(jnp.int32, shape, 0) == token) & (row < count)
    return jnp.where(hit, 1.0, 0.0).astype(jnp.bfloat16)


def decoded(codes_ref, exponents_ref):
    blocks = exponents_ref.shape[0]
    per = codes_ref.shape[0] // blocks
    parts = []
    for b in range(blocks):
        scale = jnp.exp2(exponents_ref[b].astype(jnp.float32))
        codes = codes_ref[pl.ds(b * per, per), :].astype(jnp.float32)
        parts.append((codes * scale).astype(jnp.bfloat16))
    return jnp.concatenate(parts, axis=0)


def prepare_kernel(
    slots, count, *refs
):
    weight_ref, hidden_ref, gate_factor_ref, up_factor_ref = refs[6:10]
    gate_ref, gate_exp_ref, up_ref, up_exp_ref, down_ref, down_exp_ref = refs[10:16]
    copies = fetched(refs[:6], refs[10:16], refs[16])
    for copy in copies[:4]:
        copy.wait()
    where = spread(gate_ref.shape[1], slots, count, lax.axis_index("tp"))
    gate = jnp.dot(decoded(gate_ref, gate_exp_ref), where, preferred_element_type=jnp.float32)
    up = jnp.dot(decoded(up_ref, up_exp_ref), where, preferred_element_type=jnp.float32)
    sigmoid = jax.nn.sigmoid(gate)
    silu = gate * sigmoid
    hidden_ref[...] = (silu * up).astype(jnp.bfloat16)
    gate_factor_ref[...] = up * sigmoid * (1.0 + gate * (1.0 - sigmoid))
    up_factor_ref[...] = silu
    for copy in copies[4:]:
        copy.wait()
    blocks = down_exp_ref.shape[0]
    per = down_ref.shape[0] // blocks
    for b in range(blocks):
        scale = jnp.exp2(down_exp_ref[b].astype(jnp.float32))
        codes = down_ref[pl.ds(b * per, per), :].astype(jnp.float32)
        weight_ref[pl.ds(b * per, per), :] = (codes * scale).astype(jnp.bfloat16)


def prepare(slots, count, *operands):
    units, width = operands[4].shape
    lanes = slots * TILE
    return pl.pallas_call(
        functools.partial(prepare_kernel, slots, count),
        out_shape=(
            pltpu.VMEM((units, width), jnp.bfloat16),
            pltpu.VMEM((units, lanes), jnp.bfloat16),
            pltpu.VMEM((units, lanes), jnp.float32),
            pltpu.VMEM((units, lanes), jnp.float32),
        ),
        in_specs=[LEFT] * 6,
        out_specs=[WHOLE] * 4,
        scratch_shapes=[pltpu.VMEM(operand.shape, operand.dtype) for operand in operands]
        + [pltpu.SemaphoreType.DMA((len(operands),))],
        compiler_params=PARAMS,
        cost_estimate=pl.CostEstimate(flops=4 * units * width, bytes_accessed=4 * units * width, transcendentals=0),
    )(*[pltpu.with_memory_space_constraint(operand, pltpu.HBM) for operand in operands])


def products_kernel(slots, count, chunk, *refs):
    slot_refs = refs[:slots]
    weight_ref, hidden_ref, gate_factor_ref, up_factor_ref = refs[slots : slots + 4]
    down_ref, gate_grad_ref, up_grad_ref, tile_ref, sems = refs[slots + 4 :]
    units, width = weight_ref.shape
    keep = slot_refs[0].shape[1]
    free = TILE - count
    rest = width - keep
    hidden = hidden_ref[...]
    slope = jnp.zeros((units, slots * TILE), jnp.float32)
    copies = []
    for at in range(0, width, chunk):
        parts = []
        for ref in slot_refs:
            if at < keep:
                parts.append(ref[:, at : at + chunk])
            else:
                low = ref[...][count:TILE, :]
                for j in range(count // free):
                    from_ = j * rest + at - keep
                    parts.append(low[:, from_ : from_ + chunk])
                parts.append(jnp.zeros((free, chunk), jnp.bfloat16))
        incoming = jnp.concatenate(parts, axis=0)
        down = jnp.dot(hidden, incoming, preferred_element_type=jnp.float32)
        tile_ref[:, at : at + chunk] = down.astype(jnp.bfloat16)
        copy = pltpu.make_async_copy(
            tile_ref.at[:, pl.ds(at, chunk)], down_ref.at[:, pl.ds(at, chunk)], sems.at[at // chunk]
        )
        copy.start()
        copies.append(copy)
        slope += lax.dot_general(
            weight_ref[:, at : at + chunk], incoming, (((1,), (1,)), ((), ())), preferred_element_type=jnp.float32
        )
    where = spread(gate_grad_ref.shape[1], slots, count, lax.axis_index("tp"))
    for factor_ref, grad_ref in ((gate_factor_ref, gate_grad_ref), (up_factor_ref, up_grad_ref)):
        grad = (slope * factor_ref[...]).astype(jnp.bfloat16)
        placed = lax.dot_general(grad, where, (((1,), (1,)), ((), ())), preferred_element_type=jnp.float32)
        grad_ref[...] = placed.astype(jnp.bfloat16)
    for copy in copies:
        copy.wait()


def products(got, count, weight, hidden, gate_factor, up_factor):
    slots = len(got)
    units, width = weight.shape
    tokens = slots * count
    chunk = width // 8
    return pl.pallas_call(
        functools.partial(products_kernel, slots, count, chunk),
        out_shape=(
            jax.ShapeDtypeStruct((units, width), jnp.bfloat16),
            jax.ShapeDtypeStruct((units, tokens), jnp.bfloat16),
            jax.ShapeDtypeStruct((units, tokens), jnp.bfloat16),
        ),
        in_specs=[WHOLE] * (slots + 4),
        out_specs=[LEFT, WHOLE, WHOLE],
        scratch_shapes=[
            pltpu.VMEM((units, width), jnp.bfloat16),
            pltpu.SemaphoreType.DMA((width // chunk,)),
        ],
        compiler_params=PARAMS,
        cost_estimate=pl.CostEstimate(
            flops=4 * units * width * slots * TILE, bytes_accessed=4 * units * width, transcendentals=0
        ),
    )(*got, weight, hidden, gate_factor, up_factor)


def fanned(gate_codes, gate_exponents, up_codes, up_exponents, down_codes, down_exponents, grad_held):
    n = lax.axis_size("tp")
    count = grad_held.shape[1]
    p = pack(grad_held[0])
    got = {}
    for flip in range(n - 2, -1, -2):
        got[flip] = send(p, flip, 1)
    got[1] = send(p, 1, 1)
    ready = prepare(
        n,
        count,
        gate_codes[0].T,
        gate_exponents.transpose(2, 0, 1),
        up_codes[0].T,
        up_exponents.transpose(2, 0, 1),
        down_codes[0],
        down_exponents.transpose(1, 0, 2),
    )
    for flip in range(n - 2, 0, -2):
        got[flip], _ = lax.optimization_barrier((got[flip], ready[1]))
        got[flip + 1] = send(got[flip], 1, 0)
    down_grad, gate_grad, up_grad = products([got[j] for j in range(n)], count, *ready)
    return down_grad[None], gate_grad.T[None], up_grad.T[None]


def dequantize(codes, exponents, target_axis):
    per = codes.shape[target_axis] // exponents.shape[target_axis]
    scales = jnp.exp2(jnp.repeat(exponents, per, axis=target_axis).astype(jnp.float32))
    return (codes.astype(jnp.float32) * scales).astype(jnp.bfloat16)


def ringed(gate_codes, gate_exponents, up_codes, up_exponents, down_codes, down_exponents, grad_held):
    gate = dequantize(gate_codes[0], gate_exponents[0], 1).astype(jnp.float32)
    up = dequantize(up_codes[0], up_exponents[0], 1).astype(jnp.float32)
    weight = dequantize(down_codes[0], down_exponents[0], 0)
    count = lax.axis_size("section")
    received = lax.ppermute(grad_held[0], "section", [(i, (i - 1) % count) for i in range(count)])
    incoming = lax.all_gather(received, "tp", axis=0, tiled=True)
    sigmoid = jax.nn.sigmoid(gate)
    silu = gate * sigmoid
    hidden = (silu * up).astype(jnp.bfloat16)
    down_grad = lax.dot_general(hidden, incoming, (((0,), (0,)), ((), ())), preferred_element_type=jnp.float32)
    slope = lax.dot_general(incoming, weight, (((1,), (1,)), ((), ())), preferred_element_type=jnp.float32)
    gate_grad = (slope * up * sigmoid * (1.0 + gate * (1.0 - sigmoid))).astype(jnp.bfloat16)
    up_grad = (slope * silu).astype(jnp.bfloat16)
    return down_grad.astype(jnp.bfloat16)[None], gate_grad[None], up_grad[None]


def body(*operands):
    n = lax.axis_size("tp")
    count, width = operands[-1].shape[1:]
    free = TILE - count
    small = n & (n - 1) == 0 and 2 <= n <= TILE
    fits = 0 < free < TILE and count % free == 0 and width * free % (TILE * 8 * 128) == 0
    return fanned(*operands) if small and fits else ringed(*operands)


def solution(mesh):
    wide, tall = P("section", None, "tp"), P("section", "tp", None)
    return jax.shard_map(
        body,
        mesh=mesh,
        in_specs=(wide, wide, wide, wide, tall, tall, tall),
        out_specs=(tall, wide, wide),
        check_vma=False,
    )
```

time: 44.4 us -> 27.2 us (0.61)
  blocking collectives: 33.1 us -> 0 us
  waiting for transfers between devices: 0.01 us -> 9.84 us
  starting transfers between devices: 2.43 us -> 11.7 us
  other arithmetic: 5.3 us -> 0 us
  Pallas kernels: 0 us -> 4.86 us
  matrix products: 2.04 us -> 0 us
  local copies, waits for them, and re-layouts: 0.5 us -> 0 us
    all_gather x1 -> x0, blocking collectives: 33.1 us -> none  [body(): every_row = lax.all_gather(received, 'tp', axis=0, tiled=True)]
    ppermute x1 -> x8, waiting for transfers between devices: 0.01 us -> 9.84 us  [the longest x3 6.67 us: send(): return lax.ppermute(array, 'tp', [(t, t ^ flip) for t in range(count)])]
    ppermute x1 -> x8, starting transfers between devices: 2.43 us -> 11.7 us  [the longest x5 8.68 us: send(): return lax.ppermute(array, ('section', 'tp'), pairs)]
    pallas_call x0 -> x3, Pallas kernels: none -> 4.86 us  [the longest x1 2.24 us: products(): pl.pallas_call(functools.partial(products_kernel, slots, count, chunk), o...]
    exp2 x3 -> x0, other arithmetic: 2.39 us -> none  [dequantize(): jnp.exp2(jnp.repeat(exponents, 32, axis=target_axis).astype(jnp.float32))]
    dot_general x2 -> x0, matrix products: 2.04 us -> none  [the longest x1 1.55 us: full_products(): lax.dot_general(hidden, every_row, (((0,), (0,)), ((), ())), preferred_el...]
    convert_element_type x1 -> x0, other arithmetic: 1.58 us -> none  [dequantize(): return (codes.astype(jnp.float32) * scales).astype(jnp.bfloat16)]
    broadcast_in_dim x2 -> x0, other arithmetic: 1.33 us -> none  [the longest x1 0.67 us: body(): gate_grad[None]]
  transfers between devices with their start and end apart: 1 -> 8, of which waited for: 0 -> 4; matrix products, arithmetic and copies ran while one was open for 9% -> 0% of each run, Pallas kernels for 0% -> 6%
where the time goes in v2:
time: 27.2 us; the launch traced here: 27.1 us
  starting transfers between devices  11.7 us (43%)
  waiting for transfers between devices  9.84 us (36%)
  Pallas kernels  4.86 us (18%)
  between operations  0.66 us (2%)
    ppermute x5, starting transfers between devices, send(): return lax.ppermute(array, ('section', 'tp'), pairs)  8.68 us
    ppermute x3, waiting for transfers between devices, send(): return lax.ppermute(array, 'tp', [(t, t ^ flip) for t in range(count)])  6.67 us
    ppermute x5, waiting for transfers between devices, send(): return lax.ppermute(array, ('section', 'tp'), pairs)  3.17 us
    ppermute x3, starting transfers between devices, send(): return lax.ppermute(array, 'tp', [(t, t ^ flip) for t in range(count)])  3.05 us
    pallas_call x1, Pallas kernels, products(): pl.pallas_call(functools.partial(products_kernel, slots, count, chunk), o...  2.24 us
    pallas_call x1, Pallas kernels, prepare(): pl.pallas_call(functools.partial(prepare_kernel, slots, count), out_shape...  1.69 us
    pallas_call x1, Pallas kernels, pack(): pl.pallas_call(pack_kernel, out_shape=pltpu.VMEM((TILE, width * count //...  0.93 us
  transfers between devices with their start and end apart: 8, of which 4 were waited for; matrix products, arithmetic and copies ran while one was open for 0% of the time, Pallas kernels for 6%

profile of v2, /device:TPU:0, one launch (start us, length us, event | category | flops | bytes accessed | tf_op | source)
XLA Modules:
  0.0 27.1 jit_solution(5630554605637715843)
XLA Ops:
  0.6 0.9 %shard_map.94 = bf16[16,3072]{1,0:T(8,128)(2,1)S(1)} custom-call(bf16[12,4096]{1,0:T(8,128)(2,1)} %bitcast.19), custom_call_target="tpu_custom_call" | custom-call | tf_op jit(solution)/shard_map/pallas_call | solution.py:48
  1.6 5.5 %collective-permute-start.6 = (bf16[16,3072]{1,0:T(8,128)(2,1)S(1)}, bf16[16,3072]{1,0:T(8,128)(2,1)S(1)}, u32[]{:S(2)}, u32[]{:S(2)}) collective-permute-start(bf16[16,3072]{1,0:T(8,128)(2,1)S(1)} %shard_map.94), channel_id=1, source_target_pairs={{0,30},{1,31},{2,28},{3,29},{4,26},{5,27},{6,24},{7,25},{8,6},{9,7... | collective-permute-start | bytes 294920 | tf_op jit(solution)/shard_map/ppermute | solution.py:25
  7.0 0.0 collective-permute-start.4
  7.0 0.9 %collective-permute-start.2 = (bf16[16,3072]{1,0:T(8,128)(2,1)S(1)}, bf16[16,3072]{1,0:T(8,128)(2,1)S(1)}, u32[]{:S(2)}, u32[]{:S(2)}) collective-permute-start(bf16[16,3072]{1,0:T(8,128)(2,1)S(1)} %shard_map.94), channel_id=1, source_target_pairs={{0,26},{1,27},{2,24},{3,25},{4,30},{5,31},{6,28},{7,29},{8,2},{9,3... | collective-permute-start | bytes 294920 | tf_op jit(solution)/shard_map/ppermute | solution.py:25
  7.9 1.4 %collective-permute-start.1 = (bf16[16,3072]{1,0:T(8,128)(2,1)S(1)}, bf16[16,3072]{1,0:T(8,128)(2,1)S(1)}, u32[]{:S(2)}, u32[]{:S(2)}) collective-permute-start(bf16[16,3072]{1,0:T(8,128)(2,1)S(1)} %shard_map.94), channel_id=1, source_target_pairs={{0,25},{1,24},{2,27},{3,26},{4,29},{5,28},{6,31},{7,30},{8,1},{9,0... | collective-permute-start | bytes 294920 | tf_op jit(solution)/shard_map/ppermute | solution.py:25
  9.3 0.9 %collective-permute-start = (bf16[16,3072]{1,0:T(8,128)(2,1)S(1)}, bf16[16,3072]{1,0:T(8,128)(2,1)S(1)}, u32[]{:S(2)}, u32[]{:S(2)}) collective-permute-start(bf16[16,3072]{1,0:T(8,128)(2,1)S(1)} %shard_map.94), channel_id=1, source_target_pairs={{0,24},{1,25},{2,26},{3,27},{4,28},{5,29},{6,30},{7,31},{8,0},{9,1... | collective-permute-start | bytes 294920 | tf_op jit(solution)/shard_map/ppermute | solution.py:25
  10.2 1.7 %shard_map.95 = (bf16[160,4096]{1,0:T(8,128)(2,1)S(1)}, bf16[160,128]{1,0:T(8,128)(2,1)S(1)}, f32[160,128]{1,0:T(8,128)S(1)}, f32[160,128]{1,0:T(8,128)S(1)}) custom-call(bf16[160,96]{1,0:T(8,128)(2,1)} %bitcast.21, s32[5,1,96]{2,1,0:T(1,128)} %bitcast.23, bf16[160,96]{1,0:T(8,128)(2,1)} %bitcast.22, s32[5,1,96]{2,1,0:T(1,128)} %bitcast.24, ...), custom_call_target="tpu_custom_call" | custom-call | flops 2621440 | bytes 2621440 | tf_op jit(solution)/shard_map/pallas_call | solution.py:107
  11.9 0.0 collective-permute-done.6.refs_6_
  12.0 3.2 %collective-permute-done.4.refs_4_ = bf16[16,3072]{1,0:T(8,128)(2,1)S(1)} collective-permute-done((bf16[16,3072]{1,0:T(8,128)(2,1)S(1)}, bf16[16,3072]{1,0:T(8,128)(2,1)S(1)}, u32[]{:S(2)}, u32[]{:S(2)}) %collective-permute-start.4) | collective-permute-done | bytes 98336 | tf_op jit(solution)/shard_map/ppermute | solution.py:25
  15.1 0.0 collective-permute-done.2.refs_2_
  15.1 1.0 %collective-permute-start.3 = (bf16[16,3072]{1,0:T(8,128)(2,1)S(1)}, bf16[16,3072]{1,0:T(8,128)(2,1)S(1)}, u32[]{:S(2)}, u32[]{:S(2)}) collective-permute-start(bf16[16,3072]{1,0:T(8,128)(2,1)S(1)} %collective-permute-done.2.refs_2_), channel_id=1, source_target_pairs={{0,1},{1,0},{2,3},{3,2},{4,5},{5,4},{6,7},{7,6},{8,9},{9,8},{10,11... | collective-permute-start | bytes 294920 | tf_op jit(solution)/shard_map/ppermute | solution.py:19
  16.1 1.0 %collective-permute-start.5 = (bf16[16,3072]{1,0:T(8,128)(2,1)S(1)}, bf16[16,3072]{1,0:T(8,128)(2,1)S(1)}, u32[]{:S(2)}, u32[]{:S(2)}) collective-permute-start(bf16[16,3072]{1,0:T(8,128)(2,1)S(1)} %collective-permute-done.4.refs_4_), channel_id=1, source_target_pairs={{0,1},{1,0},{2,3},{3,2},{4,5},{5,4},{6,7},{7,6},{8,9},{9,8},{10,11... | collective-permute-start | bytes 294920 | tf_op jit(solution)/shard_map/ppermute | solution.py:19
  17.1 1.0 %collective-permute-start.7 = (bf16[16,3072]{1,0:T(8,128)(2,1)S(1)}, bf16[16,3072]{1,0:T(8,128)(2,1)S(1)}, u32[]{:S(2)}, u32[]{:S(2)}) collective-permute-start(bf16[16,3072]{1,0:T(8,128)(2,1)S(1)} %collective-permute-done.6.refs_6_), channel_id=1, source_target_pairs={{0,1},{1,0},{2,3},{3,2},{4,5},{5,4},{6,7},{7,6},{8,9},{9,8},{10,11... | collective-permute-start | bytes 294920 | tf_op jit(solution)/shard_map/ppermute | solution.py:19
  18.2 0.0 collective-permute-done.1.refs_1_
  18.2 0.0 collective-permute-done.refs_0_
  18.2 2.5 %collective-permute-done.3.refs_3_ = bf16[16,3072]{1,0:T(8,128)(2,1)S(1)} collective-permute-done((bf16[16,3072]{1,0:T(8,128)(2,1)S(1)}, bf16[16,3072]{1,0:T(8,128)(2,1)S(1)}, u32[]{:S(2)}, u32[]{:S(2)}) %collective-permute-start.3) | collective-permute-done | bytes 98336 | tf_op jit(solution)/shard_map/ppermute | solution.py:19
  20.6 2.1 %collective-permute-done.5.refs_5_ = bf16[16,3072]{1,0:T(8,128)(2,1)S(1)} collective-permute-done((bf16[16,3072]{1,0:T(8,128)(2,1)S(1)}, bf16[16,3072]{1,0:T(8,128)(2,1)S(1)}, u32[]{:S(2)}, u32[]{:S(2)}) %collective-permute-start.5) | collective-permute-done | bytes 98336 | tf_op jit(solution)/shard_map/ppermute | solution.py:19
  22.7 2.1 %collective-permute-done.7.refs_7_ = bf16[16,3072]{1,0:T(8,128)(2,1)S(1)} collective-permute-done((bf16[16,3072]{1,0:T(8,128)(2,1)S(1)}, bf16[16,3072]{1,0:T(8,128)(2,1)S(1)}, u32[]{:S(2)}, u32[]{:S(2)}) %collective-permute-start.7) | collective-permute-done | bytes 98336 | tf_op jit(solution)/shard_map/ppermute | solution.py:19
  24.8 2.2 %shard_map.96 = (bf16[160,4096]{1,0:T(8,128)(2,1)}, bf16[160,96]{1,0:T(8,128)(2,1)}, bf16[160,96]{1,0:T(8,128)(2,1)}) custom-call(bf16[16,3072]{1,0:T(8,128)(2,1)S(1)} %collective-permute-done.refs_0_, bf16[16,3072]{1,0:T(8,128)(2,1)S(1)} %collective-permute-done.1.refs_1_, bf16[16,3072]{1,0:T(8,128)(2,1)S(1)} %collective-permute-done.2.refs_2_, ...), custom_call_target="tpu_custom_call" | custom-call | flops 335544320 | bytes 2621440 | tf_op jit(solution)/shard_map/pallas_call | solution.py:171
Async XLA Ops:
  1.6 10.4 %collective-permute-start.6 = (bf16[16,3072]{1,0:T(8,128)(2,1)S(1)}, bf16[16,3072]{1,0:T(8,128)(2,1)S(1)}, u32[]{:S(2)}, u32[]{:S(2)}) collective-permute-start(bf16[16,3072]{1,0:T(8,128)(2,1)S(1)} %shard_map.94), channel_id=1, source_target_pairs={{0,30},{1,31},{2,28},{3,29},{4,26},{5,27},{6,24},{7,25},{8,6},{9,7... | collective-permute-start | bytes 294920 | tf_op jit(solution)/shard_map/ppermute | solution.py:25
  7.0 8.1 %collective-permute-start.4 = (bf16[16,3072]{1,0:T(8,128)(2,1)S(1)}, bf16[16,3072]{1,0:T(8,128)(2,1)S(1)}, u32[]{:S(2)}, u32[]{:S(2)}) collective-permute-start(bf16[16,3072]{1,0:T(8,128)(2,1)S(1)} %shard_map.94), channel_id=1, source_target_pairs={{0,28},{1,29},{2,30},{3,31},{4,24},{5,25},{6,26},{7,27},{8,4},{9,5... | collective-permute-start | bytes 294920 | tf_op jit(solution)/shard_map/ppermute | solution.py:25
  7.0 8.1 %collective-permute-start.2 = (bf16[16,3072]{1,0:T(8,128)(2,1)S(1)}, bf16[16,3072]{1,0:T(8,128)(2,1)S(1)}, u32[]{:S(2)}, u32[]{:S(2)}) collective-permute-start(bf16[16,3072]{1,0:T(8,128)(2,1)S(1)} %shard_map.94), channel_id=1, source_target_pairs={{0,26},{1,27},{2,24},{3,25},{4,30},{5,31},{6,28},{7,29},{8,2},{9,3... | collective-permute-start | bytes 294920 | tf_op jit(solution)/shard_map/ppermute | solution.py:25
  7.9 10.2 %collective-permute-start.1 = (bf16[16,3072]{1,0:T(8,128)(2,1)S(1)}, bf16[16,3072]{1,0:T(8,128)(2,1)S(1)}, u32[]{:S(2)}, u32[]{:S(2)}) collective-permute-start(bf16[16,3072]{1,0:T(8,128)(2,1)S(1)} %shard_map.94), channel_id=1, source_target_pairs={{0,25},{1,24},{2,27},{3,26},{4,29},{5,28},{6,31},{7,30},{8,1},{9,0... | collective-permute-start | bytes 294920 | tf_op jit(solution)/shard_map/ppermute | solution.py:25
  9.3 8.9 %collective-permute-start = (bf16[16,3072]{1,0:T(8,128)(2,1)S(1)}, bf16[16,3072]{1,0:T(8,128)(2,1)S(1)}, u32[]{:S(2)}, u32[]{:S(2)}) collective-permute-start(bf16[16,3072]{1,0:T(8,128)(2,1)S(1)} %shard_map.94), channel_id=1, source_target_pairs={{0,24},{1,25},{2,26},{3,27},{4,28},{5,29},{6,30},{7,31},{8,0},{9,1... | collective-permute-start | bytes 294920 | tf_op jit(solution)/shard_map/ppermute | solution.py:25
  15.1 5.5 %collective-permute-start.3 = (bf16[16,3072]{1,0:T(8,128)(2,1)S(1)}, bf16[16,3072]{1,0:T(8,128)(2,1)S(1)}, u32[]{:S(2)}, u32[]{:S(2)}) collective-permute-start(bf16[16,3072]{1,0:T(8,128)(2,1)S(1)} %collective-permute-done.2.refs_2_), channel_id=1, source_target_pairs={{0,1},{1,0},{2,3},{3,2},{4,5},{5,4},{6,7},{7,6},{8,9},{9,8},{10,11... | collective-permute-start | bytes 294920 | tf_op jit(solution)/shard_map/ppermute | solution.py:19
  16.1 6.6 %collective-permute-start.5 = (bf16[16,3072]{1,0:T(8,128)(2,1)S(1)}, bf16[16,3072]{1,0:T(8,128)(2,1)S(1)}, u32[]{:S(2)}, u32[]{:S(2)}) collective-permute-start(bf16[16,3072]{1,0:T(8,128)(2,1)S(1)} %collective-permute-done.4.refs_4_), channel_id=1, source_target_pairs={{0,1},{1,0},{2,3},{3,2},{4,5},{5,4},{6,7},{7,6},{8,9},{9,8},{10,11... | collective-permute-start | bytes 294920 | tf_op jit(solution)/shard_map/ppermute | solution.py:19
  17.1 7.7 %collective-permute-start.7 = (bf16[16,3072]{1,0:T(8,128)(2,1)S(1)}, bf16[16,3072]{1,0:T(8,128)(2,1)S(1)}, u32[]{:S(2)}, u32[]{:S(2)}) collective-permute-start(bf16[16,3072]{1,0:T(8,128)(2,1)S(1)} %collective-permute-done.6.refs_6_), channel_id=1, source_target_pairs={{0,1},{1,0},{2,3},{3,2},{4,5},{5,4},{6,7},{7,6},{8,9},{9,8},{10,11... | collective-permute-start | bytes 294920 | tf_op jit(solution)/shard_map/ppermute | solution.py:19
